TPU v7x, 256 devices: a whole 4x4x8 slice. The times are simulated.
256 devices in a mesh: dp: 32 (over y, x, core), tensor: 8 (over z).
Axes of the slice: x: 4, y: 4, z: 8, core: 2. Of those that a mesh axis runs over, the one named last changes fastest.
Arguments:
- heads_out: bfloat16 [32768, 3072], P('dp', 'tensor'), may hold values from -120 to 120, as said below
- grad_out: bfloat16 [32768, 6144], P(('dp', 'tensor')), may hold values from -0.1875 to 0.1875
- error: bfloat16 [32, 3072, 6144], P('dp', 'tensor'), may hold values from -6 to 6
- q_warm: float32 [8, 64, 6144], P('tensor'), may hold values from -6 to 6
Outputs:
- p_factor: float32 [64, 3072], P(None, 'tensor')
- q_factor: float32 [8, 64, 6144], P('tensor', None, 'dp')
- error_new: bfloat16 [32, 3072, 6144], P('dp', 'tensor')
Inputs may be any that keep to these rules, and one draw needn't show every extreme that they name: `heads_out`: attention outputs of bounded magnitude.
All inputs are finite; a program needn't handle non-finite values.
Results may differ from a plain program's by a relative error of at most 0.0045.
Values may be sent and summed in bfloat16 or wider, within the bound.
A program may use at most 128 MiB of HBM per device.

v0:
```python
import functools

import jax
import jax.numpy as jnp
from jax import lax
from jax.experimental import pallas as pl
from jax.experimental.pallas import tpu as pltpu
from jax.sharding import PartitionSpec as P

MESH = pl.DeviceIdType.MESH
F32 = jnp.float32
BF16 = jnp.bfloat16


def split(value):
    high = value.astype(BF16)
    return high, (value - high.astype(F32)).astype(BF16)


def dot(a, b, a_dim, b_dim, **options):
    return lax.dot_general(a, b, (((a_dim,), (b_dim,)), ((), ())), preferred_element_type=F32, **options)


def triple(value):
    first = value.astype(BF16).astype(F32)
    rest = value - first
    second = rest.astype(BF16).astype(F32)
    return first, second, rest - second


def orthonormal(ch, rows, cols):
    place = lax.broadcasted_iota(jnp.int32, (8, 1), 0)
    tiles = range(ch.shape[1] // 128)

    def block(r, carry):
        start = pl.multiple_of(r * 8, 8)
        top = ch[pl.ds(start, 8), :]
        near = pltpu.roll(top[:, cols:], (128 - r * 8) % 128, 1)
        a = [[jnp.broadcast_to(near[i : i + 1, j : j + 1], (8, 128)) if j >= i else None for j in range(8)] for i in range(8)]
        inverse, upper = [], []
        for i in range(8):
            inverse.append(lax.rsqrt(a[i][i]))
            upper.append([a[i][j] * inverse[i] if j > i else None for j in range(8)])
            for j in range(i + 1, 8):
                for n in range(j, 8):
                    a[j][n] = a[j][n] - upper[i][j] * upper[i][n]
        done, result = [], [jnp.zeros((8, 128), F32) for _ in tiles]
        for i in range(8):
            row = [jnp.broadcast_to(top[i : i + 1, t * 128 : t * 128 + 128], (8, 128)) for t in tiles]
            for j in range(i):
                row = [row[t] - upper[j][i] * done[j][t] for t in tiles]
            row = [row[t] * inverse[i] for t in tiles]
            done.append(row)
            result = [jnp.where(place == i, row[t], result[t]) for t in tiles]
        top = jnp.concatenate(result, axis=1)
        ch[pl.ds(start, 8), :] = top
        a1, a2, a3 = triple(top[:, cols : cols + rows])
        b1, b2, b3 = triple(top)
        left = jnp.concatenate([a1, a1, a1, a2, a2, a3], axis=0).astype(BF16)
        right = jnp.concatenate([b1, b2, b3, b1, b2, b1], axis=0).astype(BF16)
        below = lax.broadcasted_iota(jnp.int32, (rows, 1), 0) >= (r + 1) * 8
        ch[...] = jnp.where(below, ch[...] - dot(left, right, 0, 0), ch[...])
        return carry

    lax.fori_loop(0, rows // 8, block, 0)


def kernel(
    sizes, heads, grad, err, q, p_out, q_out, e_out,
    own, gath, hv, at, ev, acc, qv, qs, g, pe, pt, pr, py, pf, ch,
    f, fc, xa, sa, ya, yb, sb, xb, ff, en, eh, qo, gs, gr,
    in_sem, out_sem, ring_send, ring_recv, p_send, p_recv, f_send, f_recv, c_send, c_recv, e_send, e_recv, q_send, q_recv,
):
    ny, nx, nz = sizes
    nc = 2 * ny
    bk, w = own.shape[1], own.shape[2]
    rank = qv.shape[1]
    half = rank // 2
    eighth = half // nx
    hop = nz // 2
    replicas = ny * nx * 2
    k, z = lax.axis_index("dp"), lax.axis_index("tensor")
    core, x, y = k % 2, (k // 2) % nx, k // (2 * nx)

    def at_dp(y_to, x_to, core_to):
        return ((y_to * nx + x_to) * 2 + core_to, z)

    other_core = at_dp(y, x, 1 - core)
    x_peer = [None] + [at_dp(y, (x + d) % nx, core) for d in range(1, nx)]
    y_peer = [None] + [at_dp((y + d) % ny, x, core) for d in range(1, ny)]
    row_len = 2 * nx
    row_at = x * 2 + core
    row_of = [(row_at + d) % row_len for d in range(row_len)]
    row_peer = [None] + [at_dp(y, row_of[d] // 2, row_of[d] % 2) for d in range(1, row_len)]
    z_peer = [None] + [(k, (z + d) % nz) for d in range(1, nz)]

    def remote(src, dst, send, recv, device):
        return pltpu.make_async_remote_copy(
            src_ref=src, dst_ref=dst, send_sem=send, recv_sem=recv, device_id=device, device_id_type=MESH
        )

    def loop(begin, end):
        def run(body):
            def step(c, carry):
                body(c)
                return carry

            lax.fori_loop(begin, end, step, 0)

        return run

    chunk_loop = loop(0, nc)
    window = min(4, nc // 2)

    def cols(c):
        return pl.ds(pl.multiple_of(c * w, w), w)

    def load_own(c):
        return pltpu.make_async_copy(grad.at[:, cols(c)], own.at[c], in_sem.at[0, c])

    def load_err(c):
        return pltpu.make_async_copy(err.at[0, :, cols(c)], ev.at[c], in_sem.at[1, c])

    def load_q(c):
        return pltpu.make_async_copy(q.at[0, :, cols(c)], qv.at[c], in_sem.at[2, c])

    load_heads = pltpu.make_async_copy(heads, hv, in_sem.at[3, 0])

    barrier = pltpu.get_barrier_semaphore()
    everyone = row_peer[1:] + y_peer[1:] + z_peer[1:]
    for device in everyone:
        pl.semaphore_signal(barrier, inc=1, device_id=device, device_id_type=MESH)

    load_heads.start()

    @chunk_loop
    def _(c):
        load_own(c).start()
        load_q(c).start()
        load_err(c).start()

    pl.semaphore_wait(barrier, len(everyone))

    far = 2 * (hop - 1)

    def slot(way, s):
        return way * (hop - 1) + s - 1

    def ring(way, s, c):
        part = pl.ds(way * (bk // 2), bk // 2)
        if s == 0:
            src = grad.at[:, cols(c)]
        else:
            src = gath.at[slot(way, s), c]
        if s == hop - 1:
            if s == 0:
                src = grad.at[part, cols(c)]
            else:
                src = gath.at[slot(way, s), c, part]
            dst = gath.at[far, c, part]
        else:
            dst = gath.at[slot(way, s + 1), c]
        return remote(src, dst, ring_send.at[way, s, c], ring_recv.at[way, s, c], z_peer[1] if way == 0 else z_peer[nz - 1])

    mine = pl.ds(pl.multiple_of(core * half, half), half)
    theirs = pl.ds(pl.multiple_of((1 - core) * half, half), half)

    per_chunk = nx // 2
    q_width = 2 * w // nx
    q_piece = pl.ds(pl.multiple_of((y * nx + x) * q_width, q_width), q_width)
    q_place = (2 * y + x // per_chunk, mine, pl.ds(pl.multiple_of((x % per_chunk) * q_width, q_width), q_width))
    opposite = z_peer[hop]

    def q_spread(place, first, peers):
        return [
            remote(qo.at[place], qo.at[place], q_send.at[first + d], q_recv.at[first + d], peers[d])
            for d in range(1, len(peers))
        ]

    q_over_z = remote(q.at[0, mine, q_piece], qo.at[q_place], q_send.at[0], q_recv.at[0], opposite)
    q_over_x = q_spread(q_place, 0, x_peer)
    q_over_y = q_spread((pl.ds(2 * y, 2), mine), nx - 1, y_peer)
    q_over_core = q_spread((pl.ds(0, nc), mine), nx + ny - 2, [None, other_core])
    g_over_z = remote(gs, gr, q_send.at[nx + ny], q_recv.at[nx + ny], opposite)

    q_over_z.start()

    @loop(0, window)
    def _(c):
        ring(0, 0, c).start()
        ring(1, 0, c).start()

    load_heads.wait()

    def flip(i, carry):
        at[i] = hv[pl.ds(pl.multiple_of(i * bk, bk), bk), :].astype(F32).T.astype(BF16)
        return carry

    lax.fori_loop(0, nz, flip, 0)
    g[...] = jnp.zeros_like(g)
    pe[...] = jnp.zeros_like(pe)

    def use(block, c, which):
        acc[c] += dot(at[which], block, 1, 0)

    def use_both(block, c, which):
        use(block, c, which)
        place = pl.ds(pl.multiple_of(which * bk, bk), bk)
        g[:, place] += dot(qs[c], block, 1, 1)

    def own_chunk(c):
        load_q(c).wait()
        high, low = split(qv[c])
        qs[c, 0:rank, :] = high
        qs[c, rank:, :] = low
        load_err(c).wait()
        acc[c] = ev[c].astype(F32)
        pe[...] += dot(qs[c], ev[c], 1, 1)
        load_own(c).wait()
        use_both(own[c], c, z)

    @loop(0, nc - window)
    def _(c):
        own_chunk(c)
        for way in range(2):
            ring(way, 0, c).wait_send()
            ring(way, 0, c + window).start()

    loop(nc - window, nc)(own_chunk)

    def q_step_x():
        q_over_z.wait()
        for copy in q_over_x:
            copy.start()

    def q_step_y():
        for copy in q_over_x:
            copy.wait()
        for copy in q_over_y:
            copy.start()

    def q_step_core():
        for copy in q_over_y:
            copy.wait()
        for copy in q_over_core:
            copy.start()
        for copy in q_over_core:
            copy.wait()

        def term(c, total):
            high, low = split(qo[c])
            return total + dot(jnp.concatenate([high, low], axis=0), own[c], 1, 1)

        total = lax.fori_loop(0, nc, term, jnp.zeros((2 * rank, bk), F32))
        gs[...] = total[0:rank] + total[rank:]
        g_over_z.start()

    q_step_x()
    steps = [q_step_y, q_step_core]

    def ring_chunk(s, before):
        def run(c):
            for way in range(2):
                ring(way, s - 1, c).wait_recv()
                if before is not None:
                    ring(way, *before(c)).wait_send()
                ring(way, s, c).start()
            use_both(gath[slot(0, s), c], c, (z - s + nz) % nz)
            use_both(gath[slot(1, s), c], c, (z + s) % nz)

        return run

    for s in range(1, hop):
        if s < hop - 1:
            loop(0, window)(ring_chunk(s, lambda c: (s - 1, nc - window + c)))
            loop(window, nc)(ring_chunk(s, lambda c: (s, c - window)))
        else:
            chunk_loop(ring_chunk(s, None))
        if steps:
            steps.pop(0)()
    for step in steps:
        step()
    g_over_z.wait()
    g[0:rank, pl.ds(pl.multiple_of(((z + hop) % nz) * bk, bk), bk)] = gr[...]

    def rows_of(core_at, x_at):
        return pl.ds(pl.multiple_of(core_at * half + x_at * eighth, eighth), eighth)

    rows = rows_of(core, x)

    def run_all(copies):
        for copy in copies:
            copy.start()
        for copy in copies:
            copy.wait()

    def total_of(ref, count):
        return functools.reduce(lambda a, b: a + b, [ref[i] for i in range(count)])

    total = g[0:rank, :] + g[rank:, :]
    high, low = split(total)
    terms = dot(jnp.concatenate([high, low], axis=0), hv[...], 1, 0) + pe[...]
    pt[...] = terms[0:rank, :] + terms[rank:, :]
    pr[row_at] = pt[rows, :]
    run_all([
        remote(pt.at[rows_of(row_of[d] % 2, row_of[d] // 2)], pr.at[row_at], p_send.at[0, d], p_recv.at[0, d], row_peer[d])
        for d in range(1, row_len)
    ])
    py[y] = total_of(pr, row_len)
    run_all([remote(py.at[y], py.at[y], p_send.at[1, d], p_recv.at[1, d], y_peer[d]) for d in range(1, ny)])
    pf[rows, :] = total_of(py, ny)
    run_all([remote(pf.at[rows], pf.at[rows], p_send.at[2, d], p_recv.at[2, d], row_peer[d]) for d in range(1, row_len)])

    m = pf.shape[1]
    ch[:, 0:m] = pf[...]
    ch[:, m:] = jnp.zeros((rank, 128), F32)
    ch[:, m : m + rank] = dot(pf[...], pf[...], 1, 1, precision=lax.Precision.HIGHEST)
    orthonormal(ch, rank, m)
    basis = ch[:, 0:m]
    p_out[...] = basis
    b_high, b_low = split(basis)
    b_both = jnp.concatenate([b_high, b_low], axis=0)

    per = ny // 2
    y_width = w // per
    groups = nc // 2

    def in_chunk(c):
        return pl.ds(c * per, per)

    def core_copy(c):
        return remote(f.at[in_chunk(c), theirs], fc.at[in_chunk(c)], c_send.at[c], c_recv.at[c], other_core)

    def factor_chunk(c):
        ring(0, hop - 1, c).wait_recv()
        ring(1, hop - 1, c).wait_recv()
        use(gath[far, c], c, (z + hop) % nz)
        high, low = split(acc[c])
        both = dot(b_both, high, 1, 0)
        both = (both[0:rank] + both[rank:] + dot(b_high, low, 1, 0)) * (1.0 / replicas)
        for i in range(per):
            f[c * per + i] = both[:, i * y_width : (i + 1) * y_width]
        core_copy(c).start()

    def spread(place, i, stage, peers):
        return [
            remote(ff.at[place], ff.at[place], f_send.at[i, stage, d], f_recv.at[i, stage, d], peers[d])
            for d in range(1, len(peers))
        ]

    class Group:
        def __init__(self, i):
            self.i = i
            self.base = i * ny
            self.whole = pl.ds(i * ny, ny)

        def first(self):
            i = self.i

            @loop(2 * i, 2 * i + 2)
            def _(c):
                core_copy(c).wait()

            f[self.whole, mine, :] += fc[self.whole]
            if i % 2 == 0:
                xa[i // 2, x] = f[self.whole, rows, :]
                self.copies = [
                    remote(f.at[self.whole, rows_of(core, (x + d) % nx)], xa.at[i // 2, x], f_send.at[i, 0, d], f_recv.at[i, 0, d], x_peer[d])
                    for d in range(1, nx)
                ]
            else:
                yb[i // 2, y] = f[self.base + y, mine, :]
                self.copies = [
                    remote(f.at[self.base + (y + d) % ny, mine], yb.at[i // 2, y], f_send.at[i, 0, d], f_recv.at[i, 0, d], y_peer[d])
                    for d in range(1, ny)
                ]
            self.start()

        def second(self):
            self.wait()
            i = self.i
            if i % 2 == 0:
                sa[i // 2] = total_of(xa.at[i // 2], nx)
                ya[i // 2, y] = sa[i // 2, y]
                self.copies = [
                    remote(sa.at[i // 2, (y + d) % ny], ya.at[i // 2, y], f_send.at[i, 1, d], f_recv.at[i, 1, d], y_peer[d])
                    for d in range(1, ny)
                ]
            else:
                sb[i // 2] = total_of(yb.at[i // 2], ny)

                def part(x_at):
                    return pl.ds(pl.multiple_of(x_at * eighth, eighth), eighth)

                xb[i // 2, x] = sb[i // 2, part(x), :]
                self.copies = [
                    remote(sb.at[i // 2, part((x + d) % nx)], xb.at[i // 2, x], f_send.at[i, 1, d], f_recv.at[i, 1, d], x_peer[d])
                    for d in range(1, nx)
                ]
            self.start()

        def third(self):
            self.wait()
            if self.i % 2 == 0:
                ff[self.base + y, rows, :] = total_of(ya.at[self.i // 2], ny)
            else:
                ff[self.base + y, rows, :] = total_of(xb.at[self.i // 2], nx)
            self.copies = spread((self.base + y, rows), self.i, 2, y_peer if self.i % 2 == 0 else x_peer)
            self.start()

        def fourth(self):
            self.wait()
            if self.i % 2 == 0:
                self.copies = spread((self.whole, rows), self.i, 3, x_peer)
            else:
                self.copies = spread((self.base + y, mine), self.i, 3, y_peer)
            self.start()

        def fifth(self):
            self.wait()
            self.copies = spread((self.whole, mine), self.i, 4, [None, other_core])
            self.start()

        def start(self):
            for copy in self.copies:
                copy.start()

        def wait(self):
            for copy in self.copies:
                copy.wait()

    every = [Group(i) for i in range(groups)]
    for group in every:
        loop(2 * group.i, 2 * group.i + 2)(factor_chunk)
        if group.i > 0:
            every[group.i - 1].first()
    every[-1].first()
    for step in ("second", "third", "fourth", "fifth"):
        for group in every:
            getattr(group, step)()

    def squares(i, carry):
        value = ff[i, mine, :]
        return carry + jnp.sum(value * value, axis=(0, 1), keepdims=True)

    energy = lax.fori_loop(0, nc * per, squares, jnp.zeros((1, 1), F32))
    en[z] = jnp.broadcast_to(energy, (8, 128))
    energies = [remote(en.at[z], en.at[z], e_send.at[d], e_recv.at[d], z_peer[d]) for d in range(1, nz)]
    for copy in energies:
        copy.start()

    b_wide = jnp.concatenate([b_high, b_high, b_low], axis=0).astype(F32).T.astype(BF16)

    def store(c):
        return pltpu.make_async_copy(ev.at[c], e_out.at[0, :, cols(c)], out_sem.at[c])

    def last_chunk(c):
        high, low = split(jnp.concatenate([ff[c * per + i] for i in range(per)], axis=1))
        approx = dot(b_wide, jnp.concatenate([high, low, high], axis=0), 1, 0)
        ev[c] = (acc[c] - approx).astype(BF16)
        store(c).start()

    for group in every:
        group.wait()
        loop(2 * group.i, 2 * group.i + 2)(last_chunk)

    for copy in energies:
        copy.wait()
    eh[core] = total_of(en, nz)
    run_all([remote(eh.at[core], eh.at[core], e_send.at[0], e_recv.at[0], other_core)])
    entire = (eh[0] + eh[1])[0:1, 0:1]
    scale = lax.rsqrt(entire * (1.0 / (m * nz * w * nc)) + 1e-06)
    width = q_out.shape[2]
    ahead = y_width // width
    piece = ff[k // ahead]
    piece = pltpu.roll(piece, (y_width - (k % ahead) * width) % y_width, 1)
    q_out[0] = piece[:, 0:width] * scale

    @loop(nc - window, nc)
    def _(c):
        ring(0, hop - 2, c).wait_send()
        ring(1, hop - 2, c).wait_send()

    @chunk_loop
    def _(c):
        ring(0, hop - 1, c).wait_send()
        ring(1, hop - 1, c).wait_send()

    @chunk_loop
    def _(c):
        store(c).wait()


def hand_over(p, q, e, p_out, q_out, e_out, p_held, q_held, e_held, come, go):
    parts = go.shape[0] - 2
    rows = e_held.shape[1] // parts

    def part(i):
        return (0, pl.ds(i * rows, rows))

    pairs = [(p, p_held, p_out), (q, q_held, q_out)]
    pairs += [(e.at[part(i)], e_held.at[part(i)], e_out.at[part(i)]) for i in range(parts)]
    ins = [pltpu.make_async_copy(src, held, come.at[i]) for i, (src, held, _) in enumerate(pairs)]
    outs = [pltpu.make_async_copy(held, dst, go.at[i]) for i, (_, held, dst) in enumerate(pairs)]
    for copy in ins:
        copy.start()
    for copy, onward in zip(ins, outs):
        copy.wait()
        onward.start()
    for copy in outs:
        copy.wait()


def shards(sizes, heads_out, grad_out, error, q_warm):
    ny, nx, nz = sizes
    tokens, m = heads_out.shape
    bk, width = grad_out.shape
    rank = q_warm.shape[1]
    nc = 2 * ny
    w = width // nc
    half = rank // 2
    eighth = half // nx
    hop = nz // 2
    y_width = 2 * w // ny
    count = nc * ny // 2
    pairs = (ny + 1) // 2
    dma = pltpu.SemaphoreType.DMA
    vmem = pltpu.VMEM
    hbm = pl.BlockSpec(memory_space=pl.ANY)
    outs = (
        jax.ShapeDtypeStruct((rank, m), F32),
        jax.ShapeDtypeStruct((1, rank, width // (ny * nx * 2)), F32),
        jax.ShapeDtypeStruct((1, m, width), BF16),
    )
    results = pl.pallas_call(
        functools.partial(kernel, sizes),
        out_shape=outs,
        in_specs=[hbm] * 4,
        out_specs=(pl.BlockSpec(memory_space=vmem), pl.BlockSpec(memory_space=vmem), hbm),
        scratch_shapes=[
            vmem((nc, bk, w), BF16),
            vmem((2 * (hop - 1) + 1, nc, bk, w), BF16),
            vmem((tokens, m), BF16),
            vmem((nz, m, bk), BF16),
            vmem((nc, m, w), BF16),
            vmem((nc, m, w), F32),
            vmem((nc, rank, w), F32),
            vmem((nc, 2 * rank, w), BF16),
            vmem((2 * rank, tokens), F32),
            vmem((2 * rank, m), F32),
            vmem((rank, m), F32),
            vmem((2 * nx, eighth, m), F32),
            vmem((ny, eighth, m), F32),
            vmem((rank, m), F32),
            vmem((rank, m + 128), F32),
            vmem((count, rank, y_width), F32),
            vmem((count, half, y_width), F32),
            vmem((pairs, nx, ny, eighth, y_width), F32),
            vmem((pairs, ny, eighth, y_width), F32),
            vmem((pairs, ny, eighth, y_width), F32),
            vmem((pairs, ny, half, y_width), F32),
            vmem((pairs, half, y_width), F32),
            vmem((pairs, nx, eighth, y_width), F32),
            vmem((count, rank, y_width), F32),
            vmem((nz, 8, 128), F32),
            vmem((2, 8, 128), F32),
            vmem((nc, rank, w), F32),
            vmem((rank, bk), F32),
            vmem((rank, bk), F32),
            dma((4, nc)),
            dma((nc,)),
            dma((2, hop, nc)),
            dma((2, hop, nc)),
            dma((3, max(2 * nx, ny))),
            dma((3, max(2 * nx, ny))),
            dma((nc // 2, 5, max(nx, ny))),
            dma((nc // 2, 5, max(nx, ny))),
            dma((nc,)),
            dma((nc,)),
            dma((nz,)),
            dma((nz,)),
            dma((nx + ny + 1,)),
            dma((nx + ny + 1,)),
        ],
        compiler_params=pltpu.CompilerParams(
            collective_id=0, has_side_effects=True, vmem_limit_bytes=58 * 2**20
        ),
    )(heads_out, grad_out, error, q_warm)
    parts = 6 if m % 96 == 0 else 4
    return pl.pallas_call(
        hand_over,
        out_shape=outs,
        in_specs=[hbm] * 3,
        out_specs=(hbm,) * 3,
        scratch_shapes=[vmem(out.shape, out.dtype) for out in outs] + [dma((parts + 2,)), dma((parts + 2,))],
        compiler_params=pltpu.CompilerParams(vmem_limit_bytes=60 * 2**20),
    )(*results)


def solution(mesh, ny=4, nx=4):
    placed = (
        P("dp", "tensor"),
        P(("dp", "tensor"), None),
        P("dp", "tensor", None),
        P("tensor", None, None),
    )
    return jax.shard_map(
        functools.partial(shards, (ny, nx, mesh.shape["tensor"])),
        mesh=mesh,
        in_specs=placed,
        out_specs=(P(None, "tensor"), P("tensor", None, "dp"), P("dp", "tensor", None)),
        check_vma=False,
    )
```

profile of v0, /device:TPU:1, one launch (start us, length us, event | category | flops | bytes accessed | tf_op | source)
XLA Modules:
  0.0 175.2 jit_solution(6979186180533048092)
XLA Ops:
  0.6 170.2 %shard_map.67 = (f32[64,384]{1,0:T(8,128)}, f32[1,64,192]{2,1,0:T(8,128)}, bf16[1,384,6144]{2,1,0:T(8,128)(2,1)}) custom-call(bf16[1024,384]{1,0:T(8,128)(2,1)} %heads.1, bf16[128,6144]{1,0:T(8,128)(2,1)} %grad.1, bf16[1,384,6144]{2,1,0:T(8,128)(2,1)} %err.1, f32[1,64,6144]{2,1,0:T(8,128)} %q.1), custom_call_target="tpu_custom_call" | custom-call | tf_op jit(solution)/shard_map/pallas_call | solution.py:535
  170.9 4.3 %shard_map.68 = (f32[64,384]{1,0:T(8,128)}, f32[1,64,192]{2,1,0:T(8,128)}, bf16[1,384,6144]{2,1,0:T(8,128)(2,1)}) custom-call(f32[64,384]{1,0:T(8,128)} %get-tuple-element.6.p, f32[1,64,192]{2,1,0:T(8,128)} %get-tuple-element.7.q, bf16[1,384,6144]{2,1,0:T(8,128)(2,1)} %get-tuple-element.8.e), custom_call_target="tpu_custom_call" | custom-call | tf_op jit(solution)/shard_map/pallas_call | solution.py:590
where the time goes:
time: 175 us
  Pallas kernels  175 us (100%)
    pallas_call x1, Pallas kernels, shards(): pl.pallas_call(functools.partial(kernel, sizes), out_shape=outs, in_specs...  170 us
    pallas_call x1, Pallas kernels, shards(): pl.pallas_call(hand_over, out_shape=outs, in_specs=[hbm] * 3, out_specs=(...  4.28 us

commit v1 on v0

--- a/solution.py
+++ b/solution.py
@@ -68,7 +68,7 @@
 def kernel(
     sizes, heads, grad, err, q, p_out, q_out, e_out,
     own, gath, hv, at, ev, acc, qv, qs, g, pe, pt, pr, py, pf, ch,
-    f, fc, xa, sa, ya, yb, sb, xb, ff, en, eh, qo, gs, gr,
+    f, fc, xa, sa, yb, sb, ff, en, eh, qo, gs, gr,
     in_sem, out_sem, ring_send, ring_recv, p_send, p_recv, f_send, f_recv, c_send, c_recv, e_send, e_recv, q_send, q_recv,
 ):
     ny, nx, nz = sizes
@@ -258,13 +258,16 @@
     q_step_x()
     steps = [q_step_y, q_step_core]
 
-    def ring_chunk(s, before):
+    def ring_chunk(s, before, begin=0, end=0):
         def run(c):
             for way in range(2):
                 ring(way, s - 1, c).wait_recv()
                 if before is not None:
                     ring(way, *before(c)).wait_send()
-                ring(way, s, c).start()
+                    ring(way, s, c).start()
+            for other in range(begin, end):
+                ring(0, s, other).start()
+                ring(1, s, other).start()
             use_both(gath[slot(0, s), c], c, (z - s + nz) % nz)
             use_both(gath[slot(1, s), c], c, (z + s) % nz)
 
@@ -275,7 +278,10 @@
             loop(0, window)(ring_chunk(s, lambda c: (s - 1, nc - window + c)))
             loop(window, nc)(ring_chunk(s, lambda c: (s, c - window)))
         else:
-            chunk_loop(ring_chunk(s, None))
+            late = min(3, nc - 1)
+            loop(0, nc - late)(ring_chunk(s, None))
+            for i in range(late):
+                ring_chunk(s, None, i * nc // 4, (i + 1) * nc // 4 if i < late - 1 else nc)(nc - late + i)
         if steps:
             steps.pop(0)()
     for step in steps:
@@ -317,7 +323,8 @@
     ch[:, m : m + rank] = dot(pf[...], pf[...], 1, 1, precision=lax.Precision.HIGHEST)
     orthonormal(ch, rank, m)
     basis = ch[:, 0:m]
-    p_out[...] = basis
+    basis_out = pltpu.make_async_copy(ch.at[:, pl.ds(0, m)], p_out, in_sem.at[3, 1])
+    basis_out.start()
     b_high, b_low = split(basis)
     b_both = jnp.concatenate([b_high, b_low], axis=0)
 
@@ -380,45 +387,30 @@
             self.wait()
             i = self.i
             if i % 2 == 0:
-                sa[i // 2] = total_of(xa.at[i // 2], nx)
-                ya[i // 2, y] = sa[i // 2, y]
-                self.copies = [
-                    remote(sa.at[i // 2, (y + d) % ny], ya.at[i // 2, y], f_send.at[i, 1, d], f_recv.at[i, 1, d], y_peer[d])
-                    for d in range(1, ny)
-                ]
+                sa[i // 2, y] = total_of(xa.at[i // 2], nx)
+                mine_now, peers = sa.at[i // 2, y], y_peer
             else:
-                sb[i // 2] = total_of(yb.at[i // 2], ny)
-
-                def part(x_at):
-                    return pl.ds(pl.multiple_of(x_at * eighth, eighth), eighth)
-
-                xb[i // 2, x] = sb[i // 2, part(x), :]
-                self.copies = [
-                    remote(sb.at[i // 2, part((x + d) % nx)], xb.at[i // 2, x], f_send.at[i, 1, d], f_recv.at[i, 1, d], x_peer[d])
-                    for d in range(1, nx)
-                ]
+                sb[i // 2, x] = total_of(yb.at[i // 2], ny)
+                mine_now, peers = sb.at[i // 2, x], x_peer
+            self.copies = [
+                remote(mine_now, mine_now, f_send.at[i, 1, d], f_recv.at[i, 1, d], peers[d]) for d in range(1, len(peers))
+            ]
             self.start()
 
         def third(self):
             self.wait()
-            if self.i % 2 == 0:
-                ff[self.base + y, rows, :] = total_of(ya.at[self.i // 2], ny)
+            i = self.i
+            if i % 2 == 0:
+                ff[self.whole, rows, :] = total_of(sa.at[i // 2], ny)
+                self.copies = spread((self.whole, rows), i, 2, x_peer)
             else:
-                ff[self.base + y, rows, :] = total_of(xb.at[self.i // 2], nx)
-            self.copies = spread((self.base + y, rows), self.i, 2, y_peer if self.i % 2 == 0 else x_peer)
+                ff[self.base + y, mine, :] = total_of(sb.at[i // 2], nx)
+                self.copies = spread((self.base + y, mine), i, 2, y_peer)
             self.start()
 
         def fourth(self):
             self.wait()
-            if self.i % 2 == 0:
-                self.copies = spread((self.whole, rows), self.i, 3, x_peer)
-            else:
-                self.copies = spread((self.base + y, mine), self.i, 3, y_peer)
-            self.start()
-
-        def fifth(self):
-            self.wait()
-            self.copies = spread((self.whole, mine), self.i, 4, [None, other_core])
+            self.copies = spread((self.whole, mine), self.i, 3, [None, other_core])
             self.start()
 
         def start(self):
@@ -435,7 +427,7 @@
         if group.i > 0:
             every[group.i - 1].first()
     every[-1].first()
-    for step in ("second", "third", "fourth", "fifth"):
+    for step in ("second", "third", "fourth"):
         for group in every:
             getattr(group, step)()
 
@@ -460,14 +452,16 @@
         ev[c] = (acc[c] - approx).astype(BF16)
         store(c).start()
 
+    over_core = remote(eh.at[core], eh.at[core], e_send.at[0], e_recv.at[0], other_core)
     for group in every:
         group.wait()
+        if group is every[-1]:
+            for copy in energies:
+                copy.wait()
+            eh[core] = total_of(en, nz)
+            over_core.start()
         loop(2 * group.i, 2 * group.i + 2)(last_chunk)
-
-    for copy in energies:
-        copy.wait()
-    eh[core] = total_of(en, nz)
-    run_all([remote(eh.at[core], eh.at[core], e_send.at[0], e_recv.at[0], other_core)])
+    over_core.wait()
     entire = (eh[0] + eh[1])[0:1, 0:1]
     scale = lax.rsqrt(entire * (1.0 / (m * nz * w * nc)) + 1e-06)
     width = q_out.shape[2]
@@ -489,6 +483,8 @@
     @chunk_loop
     def _(c):
         store(c).wait()
+
+    basis_out.wait()
 
 
 def hand_over(p, q, e, p_out, q_out, e_out, p_held, q_held, e_held, come, go):
@@ -536,7 +532,7 @@
         functools.partial(kernel, sizes),
         out_shape=outs,
         in_specs=[hbm] * 4,
-        out_specs=(pl.BlockSpec(memory_space=vmem), pl.BlockSpec(memory_space=vmem), hbm),
+        out_specs=(hbm, pl.BlockSpec(memory_space=vmem), hbm),
         scratch_shapes=[
             vmem((nc, bk, w), BF16),
             vmem((2 * (hop - 1) + 1, nc, bk, w), BF16),
@@ -556,11 +552,9 @@
             vmem((count, rank, y_width), F32),
             vmem((count, half, y_width), F32),
             vmem((pairs, nx, ny, eighth, y_width), F32),
-            vmem((pairs, ny, eighth, y_width), F32),
-            vmem((pairs, ny, eighth, y_width), F32),
+            vmem((pairs, ny, ny, eighth, y_width), F32),
             vmem((pairs, ny, half, y_width), F32),
-            vmem((pairs, half, y_width), F32),
-            vmem((pairs, nx, eighth, y_width), F32),
+            vmem((pairs, nx, half, y_width), F32),
             vmem((count, rank, y_width), F32),
             vmem((nz, 8, 128), F32),
             vmem((2, 8, 128), F32),
@@ -573,8 +567,8 @@
             dma((2, hop, nc)),
             dma((3, max(2 * nx, ny))),
             dma((3, max(2 * nx, ny))),
-            dma((nc // 2, 5, max(nx, ny))),
-            dma((nc // 2, 5, max(nx, ny))),
+            dma((nc // 2, 4, max(nx, ny))),
+            dma((nc // 2, 4, max(nx, ny))),
             dma((nc,)),
             dma((nc,)),
             dma((nz,)),

time: 175 us -> 173 us (0.989)
  Pallas kernels: 175 us -> 172 us
    pallas_call x1, Pallas kernels: 170 us -> 168 us  [shards(): pl.pallas_call(functools.partial(kernel, sizes), out_shape=outs, in_specs...]
where the time goes in v1:
time: 173 us; the launch traced here: 172 us
  Pallas kernels  172 us (99%)
    pallas_call x1, Pallas kernels, shards(): pl.pallas_call(functools.partial(kernel, sizes), out_shape=outs, in_specs...  168 us
    pallas_call x1, Pallas kernels, shards(): pl.pallas_call(hand_over, out_shape=outs, in_specs=[hbm] * 3, out_specs=(...  4.28 us

profile of v1, /device:TPU:1, one launch (start us, length us, event | category | flops | bytes accessed | tf_op | source)
XLA Modules:
  0.0 172.4 jit_solution(15537196506941537951)
XLA Ops:
  0.6 167.5 %shard_map.67 = (f32[64,384]{1,0:T(8,128)}, f32[1,64,192]{2,1,0:T(8,128)}, bf16[1,384,6144]{2,1,0:T(8,128)(2,1)}) custom-call(bf16[1024,384]{1,0:T(8,128)(2,1)} %heads.1, bf16[128,6144]{1,0:T(8,128)(2,1)} %grad.1, bf16[1,384,6144]{2,1,0:T(8,128)(2,1)} %err.1, f32[1,64,6144]{2,1,0:T(8,128)} %q.1), custom_call_target="tpu_custom_call" | custom-call | tf_op jit(solution)/shard_map/pallas_call | solution.py:531
  168.2 4.3 %shard_map.68 = (f32[64,384]{1,0:T(8,128)}, f32[1,64,192]{2,1,0:T(8,128)}, bf16[1,384,6144]{2,1,0:T(8,128)(2,1)}) custom-call(f32[64,384]{1,0:T(8,128)} %get-tuple-element.6.p, f32[1,64,192]{2,1,0:T(8,128)} %get-tuple-element.7.q, bf16[1,384,6144]{2,1,0:T(8,128)(2,1)} %get-tuple-element.8.e), custom_call_target="tpu_custom_call" | custom-call | tf_op jit(solution)/shard_map/pallas_call | solution.py:584

commit v2 on v1

--- a/solution.py
+++ b/solution.py
@@ -355,6 +355,10 @@
             for d in range(1, len(peers))
         ]
 
+    def squares(i, carry):
+        value = ff[i, mine, :]
+        return carry + jnp.sum(value * value, axis=(0, 1), keepdims=True)
+
     class Group:
         def __init__(self, i):
             self.i = i
@@ -410,6 +414,7 @@
 
         def fourth(self):
             self.wait()
+            self.energy = lax.fori_loop(self.base, self.base + ny, squares, jnp.zeros((1, 1), F32))
             self.copies = spread((self.whole, mine), self.i, 3, [None, other_core])
             self.start()
 
@@ -427,19 +432,10 @@
         if group.i > 0:
             every[group.i - 1].first()
     every[-1].first()
-    for step in ("second", "third", "fourth"):
-        for group in every:
-            getattr(group, step)()
-
-    def squares(i, carry):
-        value = ff[i, mine, :]
-        return carry + jnp.sum(value * value, axis=(0, 1), keepdims=True)
-
-    energy = lax.fori_loop(0, nc * per, squares, jnp.zeros((1, 1), F32))
-    en[z] = jnp.broadcast_to(energy, (8, 128))
-    energies = [remote(en.at[z], en.at[z], e_send.at[d], e_recv.at[d], z_peer[d]) for d in range(1, nz)]
-    for copy in energies:
-        copy.start()
+    for group in every:
+        group.second()
+    for group in every:
+        group.third()
 
     b_wide = jnp.concatenate([b_high, b_high, b_low], axis=0).astype(F32).T.astype(BF16)
 
@@ -452,16 +448,26 @@
         ev[c] = (acc[c] - approx).astype(BF16)
         store(c).start()
 
-    over_core = remote(eh.at[core], eh.at[core], e_send.at[0], e_recv.at[0], other_core)
-    for group in every:
+    def finish(group):
         group.wait()
-        if group is every[-1]:
-            for copy in energies:
-                copy.wait()
-            eh[core] = total_of(en, nz)
-            over_core.start()
         loop(2 * group.i, 2 * group.i + 2)(last_chunk)
-    over_core.wait()
+
+    for group in every[:-1]:
+        group.fourth()
+        if group.i > 0:
+            finish(every[group.i - 1])
+    every[-1].fourth()
+    energy = functools.reduce(lambda a, b: a + b, [group.energy for group in every])
+    en[z] = jnp.broadcast_to(energy, (8, 128))
+    energies = [remote(en.at[z], en.at[z], e_send.at[d], e_recv.at[d], z_peer[d]) for d in range(1, nz)]
+    for copy in energies:
+        copy.start()
+    for group in every[max(groups - 2, 0) :]:
+        finish(group)
+    for copy in energies:
+        copy.wait()
+    eh[core] = total_of(en, nz)
+    run_all([remote(eh.at[core], eh.at[core], e_send.at[0], e_recv.at[0], other_core)])
     entire = (eh[0] + eh[1])[0:1, 0:1]
     scale = lax.rsqrt(entire * (1.0 / (m * nz * w * nc)) + 1e-06)
     width = q_out.shape[2]

time: 173 us -> 172 us (level)
  no operation moved by 1% of the time
where the time goes in v2:
time: 172 us; the launch traced here: 171 us
  Pallas kernels  171 us (99%)
    pallas_call x1, Pallas kernels, shards(): pl.pallas_call(functools.partial(kernel, sizes), out_shape=outs, in_specs...  167 us
    pallas_call x1, Pallas kernels, shards(): pl.pallas_call(hand_over, out_shape=outs, in_specs=[hbm] * 3, out_specs=(...  4.28 us

profile of v2, /device:TPU:1, one launch (start us, length us, event | category | flops | bytes accessed | tf_op | source)
XLA Modules:
  0.0 171.5 jit_solution(9275417340498385029)
XLA Ops:
  0.6 166.6 %shard_map.67 = (f32[64,384]{1,0:T(8,128)}, f32[1,64,192]{2,1,0:T(8,128)}, bf16[1,384,6144]{2,1,0:T(8,128)(2,1)}) custom-call(bf16[1024,384]{1,0:T(8,128)(2,1)} %heads.1, bf16[128,6144]{1,0:T(8,128)(2,1)} %grad.1, bf16[1,384,6144]{2,1,0:T(8,128)(2,1)} %err.1, f32[1,64,6144]{2,1,0:T(8,128)} %q.1), custom_call_target="tpu_custom_call" | custom-call | tf_op jit(solution)/shard_map/pallas_call | solution.py:537
  167.2 4.3 %shard_map.68 = (f32[64,384]{1,0:T(8,128)}, f32[1,64,192]{2,1,0:T(8,128)}, bf16[1,384,6144]{2,1,0:T(8,128)(2,1)}) custom-call(f32[64,384]{1,0:T(8,128)} %get-tuple-element.6.p, f32[1,64,192]{2,1,0:T(8,128)} %get-tuple-element.7.q, bf16[1,384,6144]{2,1,0:T(8,128)(2,1)} %get-tuple-element.8.e), custom_call_target="tpu_custom_call" | custom-call | tf_op jit(solution)/shard_map/pallas_call | solution.py:590

commit v3 on v2

--- a/solution.py
+++ b/solution.py
@@ -99,13 +99,13 @@
             src_ref=src, dst_ref=dst, send_sem=send, recv_sem=recv, device_id=device, device_id_type=MESH
         )
 
-    def loop(begin, end):
+    def loop(begin, end, unroll=1):
         def run(body):
             def step(c, carry):
                 body(c)
                 return carry
 
-            lax.fori_loop(begin, end, step, 0)
+            lax.fori_loop(begin, end, step, 0, unroll=unroll)
 
         return run
 
@@ -294,9 +294,16 @@
 
     rows = rows_of(core, x)
 
-    def run_all(copies):
+    def far_chunk(c):
+        ring(0, hop - 1, c).wait_recv()
+        ring(1, hop - 1, c).wait_recv()
+        use(gath[far, c], c, (z + hop) % nz)
+
+    def run_all(copies, meanwhile=None):
         for copy in copies:
             copy.start()
+        if meanwhile is not None:
+            meanwhile(far_chunk)
         for copy in copies:
             copy.wait()
 
@@ -313,9 +320,9 @@
         for d in range(1, row_len)
     ])
     py[y] = total_of(pr, row_len)
-    run_all([remote(py.at[y], py.at[y], p_send.at[1, d], p_recv.at[1, d], y_peer[d]) for d in range(1, ny)])
+    run_all([remote(py.at[y], py.at[y], p_send.at[1, d], p_recv.at[1, d], y_peer[d]) for d in range(1, ny)], loop(0, nc // 4))
     pf[rows, :] = total_of(py, ny)
-    run_all([remote(pf.at[rows], pf.at[rows], p_send.at[2, d], p_recv.at[2, d], row_peer[d]) for d in range(1, row_len)])
+    run_all([remote(pf.at[rows], pf.at[rows], p_send.at[2, d], p_recv.at[2, d], row_peer[d]) for d in range(1, row_len)], loop(nc // 4, nc // 2))
 
     m = pf.shape[1]
     ch[:, 0:m] = pf[...]
@@ -338,10 +345,9 @@
     def core_copy(c):
         return remote(f.at[in_chunk(c), theirs], fc.at[in_chunk(c)], c_send.at[c], c_recv.at[c], other_core)
 
-    def factor_chunk(c):
-        ring(0, hop - 1, c).wait_recv()
-        ring(1, hop - 1, c).wait_recv()
-        use(gath[far, c], c, (z + hop) % nz)
+    def factor_chunk(c, early):
+        if not early:
+            far_chunk(c)
         high, low = split(acc[c])
         both = dot(b_both, high, 1, 0)
         both = (both[0:rank] + both[rank:] + dot(b_high, low, 1, 0)) * (1.0 / replicas)
@@ -428,7 +434,7 @@
 
     every = [Group(i) for i in range(groups)]
     for group in every:
-        loop(2 * group.i, 2 * group.i + 2)(factor_chunk)
+        loop(2 * group.i, 2 * group.i + 2, 2)(functools.partial(factor_chunk, early=group.i < groups // 2))
         if group.i > 0:
             every[group.i - 1].first()
     every[-1].first()
@@ -450,7 +456,7 @@
 
     def finish(group):
         group.wait()
-        loop(2 * group.i, 2 * group.i + 2)(last_chunk)
+        loop(2 * group.i, 2 * group.i + 2, 2)(last_chunk)
 
     for group in every[:-1]:
         group.fourth()

time: 172 us -> 171 us (level)
  no operation moved by 1% of the time
where the time goes in v3:
time: 171 us
  Pallas kernels  170 us (99%)
    pallas_call x1, Pallas kernels, shards(): pl.pallas_call(functools.partial(kernel, sizes), out_shape=outs, in_specs...  166 us
    pallas_call x1, Pallas kernels, shards(): pl.pallas_call(hand_over, out_shape=outs, in_specs=[hbm] * 3, out_specs=(...  4.28 us

profile of v3, /device:TPU:1, one launch (start us, length us, event | category | flops | bytes accessed | tf_op | source)
XLA Modules:
  0.0 171.0 jit_solution(4970231473417859821)
XLA Ops:
  0.6 166.1 %shard_map.67 = (f32[64,384]{1,0:T(8,128)}, f32[1,64,192]{2,1,0:T(8,128)}, bf16[1,384,6144]{2,1,0:T(8,128)(2,1)}) custom-call(bf16[1024,384]{1,0:T(8,128)(2,1)} %heads.1, bf16[128,6144]{1,0:T(8,128)(2,1)} %grad.1, bf16[1,384,6144]{2,1,0:T(8,128)(2,1)} %err.1, f32[1,64,6144]{2,1,0:T(8,128)} %q.1), custom_call_target="tpu_custom_call" | custom-call | tf_op jit(solution)/shard_map/pallas_call | solution.py:543
  166.7 4.3 %shard_map.68 = (f32[64,384]{1,0:T(8,128)}, f32[1,64,192]{2,1,0:T(8,128)}, bf16[1,384,6144]{2,1,0:T(8,128)(2,1)}) custom-call(f32[64,384]{1,0:T(8,128)} %get-tuple-element.6.p, f32[1,64,192]{2,1,0:T(8,128)} %get-tuple-element.7.q, bf16[1,384,6144]{2,1,0:T(8,128)(2,1)} %get-tuple-element.8.e), custom_call_target="tpu_custom_call" | custom-call | tf_op jit(solution)/shard_map/pallas_call | solution.py:596
